TPU v7x, 256 devices: a whole 4x4x8 slice. The times are simulated.
256 devices in a mesh: dp: 16 (over x_hi, y, core), blk: 16 (over z, x_lo).
Axes of the slice: x: 4 (x_hi: 2, x_lo: 2; x = x_hi * 2 + x_lo), y: 4, z: 8, core: 2. Of those that a mesh axis runs over, the one named last changes fastest.
Arguments:
- rows_in: bfloat16 [16, 16, 16, 16, 4608], P('dp', 'blk'), may hold values from -8 to 8, as said below
- slot_rows: int32 [16, 16, 16, 16], P('dp', 'blk'), may hold values from 0 to 128, as said below
- clip_ids: int32 [16, 2048], P('dp'), may hold values from 0 to 3, never falling along the last dimension, each value on 1 to 2036 neighbouring positions
- clip_reach: int32 [16, 4], P('dp'), may hold values from 0 to 3
- clip_step: int32 [16, 4], P('dp'), may hold values from 0 to 63
- gate_table: bfloat16 [64, 1536], replicated, may hold values from -4 to 4
- out_grad: bfloat16 [16, 2048, 1536], P('dp', 'blk'), may hold values from -6 to 6
Outputs:
- attended: bfloat16 [16, 2048, 1536], P('dp', 'blk')
- qkv_grad: bfloat16 [16, 2048, 4608], P('dp', 'blk')
- gate_grad: float32 [64, 1536], replicated
Inputs may be any that keep to these rules, and one draw needn't show every extreme that they name: `rows_in`: each row holds one token's query, key and value columns, 12 heads of 128 side by side in each. For every q and b, the entries below 128 of slot_rows[:, b, q, :] name each of 0 to 127 exactly once; 128 marks an empty slot.
All inputs are finite; a program needn't handle non-finite values.
Results may differ from a plain program's by a relative error of at most 0.023.
Values may be sent and summed in bfloat16 or wider, within the bound.
A program may use at most 128 MiB of HBM per device.

v0:
```python
import math

import jax
import jax.numpy as jnp
from jax import lax
from jax.sharding import PartitionSpec as P

HEAD = 128
FRAME = 128


NEGATIVE = -1e30


def clip_layout(clip_row, reach_row, step_row, frame):
    clip_count = reach_row.shape[0]
    onehot = clip_row[:, None] == jnp.arange(clip_count, dtype=jnp.int32)[None, :]
    counts = jnp.sum(onehot.astype(jnp.int32), axis=0)
    starts = jnp.cumsum(counts) - counts
    clip_first = jnp.sum(jnp.where(onehot, starts[None, :], 0), axis=1)
    positions = jnp.arange(clip_row.shape[0], dtype=jnp.int32) - clip_first
    mask_block = positions // frame
    row_reach = jnp.sum(jnp.where(onehot, reach_row[None, :], 0), axis=1)
    row_step = jnp.sum(jnp.where(onehot, step_row[None, :], 0), axis=1)
    return (mask_block, row_reach, row_step)


def allowed_pairs(row_clip, row_block, row_reach, col_clip, col_block):
    same_clip = row_clip[:, None] == col_clip[None, :]
    return same_clip & (col_block[None, :] <= row_block[:, None] + row_reach[:, None])


def head_scores(row_cols, col_cols, group_heads):
    left_side = row_cols.reshape(row_cols.shape[0], group_heads, HEAD)
    right_side = col_cols.reshape(col_cols.shape[0], group_heads, HEAD)
    return jnp.einsum("rhd,khd->hrk", left_side, right_side, preferred_element_type=jnp.float32)


def local(rows_in, slot_rows, clip_ids, clip_reach, clip_step, gate_table, out_grad):
    step_count, row_width = gate_table.shape
    tok_rows = out_grad.shape[1]
    head_count = row_width // HEAD
    group_heads = math.gcd(head_count, 4)
    group_span = group_heads * HEAD
    group_total = head_count // group_heads
    score_scale = 1.0 / math.sqrt(HEAD)
    received, places = (
        lax.all_to_all(rows_in, "dp", split_axis=2, concat_axis=0, tiled=True),
        lax.all_to_all(slot_rows, "dp", split_axis=2, concat_axis=0, tiled=True),
    )
    slot_count = received.shape[0] * received.shape[3]
    received = received.reshape(slot_count, 3 * row_width)
    places = places.reshape(slot_count)
    placing = (places[None, :] == jnp.arange(tok_rows, dtype=jnp.int32)[:, None]).astype(
        jnp.bfloat16
    )
    packed = jnp.dot(placing, received, preferred_element_type=jnp.float32).astype(jnp.bfloat16)
    queries = packed[:, :row_width]
    key_value = packed[:, row_width:]
    clip_row = clip_ids[0]
    seq_len = clip_row.shape[0]
    mask_block, row_reach, row_step = clip_layout(clip_row, clip_reach[0], clip_step[0], FRAME)
    row_offset = lax.axis_index("blk") * tok_rows

    def own_rows(values):
        return lax.dynamic_slice_in_dim(values, row_offset, tok_rows, 0)

    own_clip = own_rows(clip_row)
    own_block = own_rows(mask_block)
    own_reach = own_rows(row_reach)
    own_step = own_rows(row_step)
    step_hot = (own_step[:, None] == jnp.arange(step_count, dtype=jnp.int32)[None, :]).astype(
        jnp.float32
    )
    gate_rows = jnp.dot(step_hot, gate_table.astype(jnp.float32), precision=lax.Precision.HIGHEST)
    grad_float = out_grad[0].astype(jnp.float32)
    grad_out = (gate_rows * grad_float).astype(jnp.bfloat16)
    query_mask = allowed_pairs(own_clip, own_block, own_reach, clip_row, mask_block)
    all_keys = lax.all_gather(key_value, "blk", axis=0, tiled=True)
    totals_list, outputs, kept = ([], [], [])
    for number in range(group_total):
        column_low = number * group_span
        scores = (
            head_scores(
                queries[:, column_low : column_low + group_span],
                all_keys[:, column_low : column_low + group_span],
                group_heads,
            )
            * score_scale
        )
        scores = jnp.where(query_mask[None], scores, NEGATIVE)
        row_top = jnp.max(scores, axis=2)
        log_total = row_top + jnp.log(jnp.sum(jnp.exp(scores - row_top[:, :, None]), axis=2))
        weights = jnp.where(query_mask[None], jnp.exp(scores - log_total[:, :, None]), 0.0)
        values_group = all_keys[
            :, row_width + column_low : row_width + column_low + group_span
        ].reshape(seq_len, group_heads, HEAD)
        summed = jnp.einsum(
            "hrk,khd->rhd",
            weights.astype(jnp.bfloat16),
            values_group,
            preferred_element_type=jnp.float32,
        )
        outputs.append(summed.reshape(tok_rows, group_span))
        totals_list.append(log_total)
        kept.append(weights)
    log_totals = jnp.concatenate(totals_list, axis=0)
    attention = jnp.concatenate(outputs, axis=1)
    row_delta = jnp.sum(
        (grad_out.astype(jnp.float32) * attention).reshape(tok_rows, head_count, HEAD), axis=2
    )
    delta_heads = row_delta.T
    query_parts = []
    for number in range(group_total):
        column_low = number * group_span
        heads_low = number * group_heads
        keys_group = all_keys[:, column_low : column_low + group_span].reshape(
            seq_len, group_heads, HEAD
        )
        values_group = all_keys[
            :, row_width + column_low : row_width + column_low + group_span
        ].reshape(seq_len, group_heads, HEAD)
        grad_group = grad_out[:, column_low : column_low + group_span].reshape(
            tok_rows, group_heads, HEAD
        )
        prob_grad = jnp.einsum(
            "rhd,khd->hrk", grad_group, values_group, preferred_element_type=jnp.float32
        )
        score_grad = (
            kept[number]
            * (prob_grad - delta_heads[heads_low : heads_low + group_heads][:, :, None])
        ).astype(jnp.bfloat16)
        query_term = jnp.einsum(
            "hrk,khd->rhd", score_grad, keys_group, preferred_element_type=jnp.float32
        )
        query_parts.append(query_term.reshape(tok_rows, group_span) * score_scale)
    query_grad = jnp.concatenate(query_parts, axis=1)
    query_block = lax.all_gather(queries.astype(jnp.float32), "blk", axis=0, tiled=True).astype(
        jnp.bfloat16
    )
    grad_block = lax.all_gather(grad_out.astype(jnp.float32), "blk", axis=0, tiled=True).astype(
        jnp.bfloat16
    )
    total_block = lax.all_gather(log_totals.T, "blk", axis=0, tiled=True)
    delta_block = lax.all_gather(row_delta, "blk", axis=0, tiled=True)
    count_rows = query_block.shape[0]
    allowed = allowed_pairs(clip_row, mask_block, row_reach, own_clip, own_block)
    key_parts = []
    value_parts = []
    for number in range(group_total):
        column_low = number * group_span
        heads_low = number * group_heads
        query_group = query_block[:, column_low : column_low + group_span].reshape(
            count_rows, group_heads, HEAD
        )
        grad_group = grad_block[:, column_low : column_low + group_span].reshape(
            count_rows, group_heads, HEAD
        )
        keys_group = key_value[:, column_low : column_low + group_span].reshape(
            tok_rows, group_heads, HEAD
        )
        values_group = key_value[
            :, row_width + column_low : row_width + column_low + group_span
        ].reshape(tok_rows, group_heads, HEAD)
        scores = (
            jnp.einsum("rhd,khd->hrk", query_group, keys_group, preferred_element_type=jnp.float32)
            * score_scale
        )
        scores = jnp.where(allowed[None], scores, NEGATIVE)
        weights = jnp.where(
            allowed[None],
            jnp.exp(scores - total_block[:, heads_low : heads_low + group_heads].T[:, :, None]),
            0.0,
        )
        value_term = jnp.einsum(
            "hrk,rhd->khd",
            weights.astype(jnp.bfloat16),
            grad_group,
            preferred_element_type=jnp.float32,
        )
        value_parts.append(value_term.reshape(tok_rows, group_span))
        prob_grad = jnp.einsum(
            "rhd,khd->hrk", grad_group, values_group, preferred_element_type=jnp.float32
        )
        score_grad = (
            weights
            * (prob_grad - delta_block[:, heads_low : heads_low + group_heads].T[:, :, None])
        ).astype(jnp.bfloat16)
        key_term = jnp.einsum(
            "hrk,rhd->khd", score_grad, query_group, preferred_element_type=jnp.float32
        )
        key_parts.append(key_term.reshape(tok_rows, group_span))
    key_sum = jnp.concatenate(key_parts, axis=1)
    value_sum = jnp.concatenate(value_parts, axis=1)
    qkv_grad = jnp.concatenate([query_grad, key_sum * score_scale, value_sum], axis=1).astype(
        jnp.bfloat16
    )[None]
    attended = (gate_rows * attention).astype(jnp.bfloat16)[None]
    gate_term = jnp.dot(step_hot.T, grad_float * attention, precision=lax.Precision.HIGHEST)
    gate_grad = lax.psum(gate_term, ("dp", "blk"))
    return (attended, qkv_grad, gate_grad)


def solution(mesh):
    return jax.shard_map(
        local,
        mesh=mesh,
        in_specs=(
            P("dp", "blk", None, None, None),
            P("dp", "blk", None, None),
            P("dp", None),
            P("dp", None),
            P("dp", None),
            P(),
            P("dp", "blk", None),
        ),
        out_specs=(P("dp", "blk", None), P("dp", "blk", None), P()),
        check_vma=False,
    )
```

profile of v0, /device:TPU:1, one launch (start us, length us, event | category | flops | bytes accessed | tf_op | source)
XLA Modules:
  0.0 889.9 jit_solution(6138877882930695589)
XLA Ops:
  7.2 15.5 %all_to_all.8 = s32[1,1,16,16]{3,1,0,2:T(1,128)S(1)} all-to-all(s32[1,1,16,16]{3,1,0,2:T(1,128)} %bitcast.256), channel_id=1, replica_groups=mesh['dp'=16,'blk'=16] {'dp'}, dimensions={2} | all-to-all | bytes 2048 | tf_op jit(solution)/shard_map/all_to_all | solution.py:49
  22.7 4.2 all-to-all-start.1
  28.2 30.4 %all-to-all-done.1 = bf16[1,1,16,16,4608]{4,3,1,0,2:T(8,128)(2,1)S(1)} async-done(((bf16[1,1,16,16,4608]{4,3,1,0,2:T(8,128)(2,1)}), bf16[1,1,16,16,4608]{4,3,1,0,2:T(8,128)(2,1)S(1)}, u32[]{:S(2)}, u32[]{:S(2)}) %all-to-all-start.1) | async-done | bytes 2359328 | tf_op jit(solution)/shard_map/all_to_all | solution.py:48
  65.9 267.2 %all-gather.4.cloned.1.call-done = bf16[2048,3072]{1,0:T(8,128)(2,1)} async-done(((bf16[128,3072]{1,0:T(8,128)(2,1)}), bf16[2048,3072]{1,0:T(8,128)(2,1)}) %all-gather.4.cloned.1.call-update) | async-done | bytes 12582928 | tf_op jit(solution)/shard_map/all_gather | solution.py:79
  333.1 9.2 %slice_bitcast_fusion.2 = (bf16[256,4,8,128]{3,2,1,0:T(8,128)(2,1)}, bf16[2048,512]{1,0:T(8,128)(2,1)}, bf16[256,4,8,128]{3,2,1,0:T(8,128)(2,1)}, bf16[2048,512]...) fusion(bf16[2048,3072]{1,0:T(8,128)(2,1)} %all-gather.4.cloned.1.call-done), kind=kLoop, calls=%fused_computation.33 | loop fusion | bytes 25165824
  342.3 3.9 copy.241
  346.3 4.0 copy.240
  361.7 4.0 fusion.5
  379.5 98.3 %all-gather.6.cloned.1.call-done = bf16[2048,1536]{1,0:T(8,128)(2,1)} async-done(((bf16[128,1536]{1,0:T(8,128)(2,1)}), bf16[2048,1536]{1,0:T(8,128)(2,1)}) %all-gather.6.cloned.1.call-update) | async-done | bytes 6291472 | tf_op jit(solution)/shard_map/all_gather | solution.py:138
  477.8 5.4 fusion.135
  483.1 4.0 copy.246
  487.1 4.0 copy.244
  498.1 4.9 fusion.66
  503.1 5.5 fusion.69
  508.8 5.5 fusion.72
  515.5 30.8 %all_gather.19 = f32[2048,12]{0,1:T(8,128)S(1)} all-gather(f32[128,12]{0,1:T(8,128)S(1)} %reduce_sum.79), channel_id=1, replica_groups=mesh['dp'=16,'blk'=16] {'blk'}, dimensions={0}, use_global_device_ids=true | all-gather | bytes 104448 | tf_op jit(solution)/shard_map/all_gather | solution.py:145
  546.3 30.0 %all_gather.17 = f32[2048,12]{0,1:T(8,128)} all-gather(f32[128,12]{0,1:T(8,128)S(1)} %maximum_bitcast_fusion), channel_id=1, replica_groups=mesh['dp'=16,'blk'=16] {'blk'}, dimensions={0}, use_global_device_ids=true | all-gather | bytes 104448 | tf_op jit(solution)/shard_map/all_gather | solution.py:144
  580.7 5.2 exponential_select_fusion
  586.0 3.6 exponential_select_fusion.1
  589.6 3.6 exponential_select_fusion.2
  593.2 33.1 %all-gather.8.cloned.1.call-done = bf16[2048,1536]{1,0:T(8,128)(2,1)} async-done(((bf16[128,1536]{1,0:T(8,128)(2,1)}), bf16[2048,1536]{1,0:T(8,128)(2,1)}) %all-gather.8.cloned.1.call-update) | async-done | bytes 6291472 | tf_op jit(solution)/shard_map/all_gather | solution.py:141
  626.3 5.6 fusion.134
  631.9 2.9 copy.247
  634.8 2.9 fusion.63
  637.8 4.7 fusion.38
  642.7 2.9 copy.245
  645.6 2.9 fusion.60
  648.6 4.8 fusion.37
  653.5 2.9 copy.243
  656.4 3.6 fusion.57
  660.0 4.8 fusion.36
  669.1 212.6 %all-reduce.2.cloned.1.call-done = f32[64,1536]{1,0:T(8,128)} async-done(((f32[64,1536]{1,0:T(8,128)}), f32[64,1536]{1,0:T(8,128)}) %all-reduce.2.cloned.1.call-update) | async-done | bytes 393232 | tf_op jit(solution)/shard_map/psum | solution.py:200
  (124 shorter events, 52.5 us)
Async XLA Ops:
  7.2 368.4 %copy-start = (bf16[64,1536]{1,0:T(8,128)(2,1)S(1)}, bf16[64,1536]{1,0:T(8,128)(2,1)}, u32[]{:S(2)}) copy-start(bf16[64,1536]{1,0:T(8,128)(2,1)} %param.12) | copy-start | bytes 589828
  22.7 35.9 %all-to-all-start.1 = ((bf16[1,1,16,16,4608]{4,3,1,0,2:T(8,128)(2,1)}), bf16[1,1,16,16,4608]{4,3,1,0,2:T(8,128)(2,1)S(1)}, u32[]{:S(2)}, u32[]{:S(2)}) async-start(bf16[1,1,16,16,4608]{4,3,1,0,2:T(8,128)(2,1)} %bitcast.238), calls=%async_computation.1 | async-start | bytes 4718592 | tf_op jit(solution)/shard_map/all_to_all | solution.py:48
  26.9 306.3 %all-gather.4.cloned.1.call-start = ((), (), s32[]{:S(2)}) async-start(), calls=%async_computation.2 | async-start | bytes 13369344 | tf_op jit(solution)/shard_map/all_gather | solution.py:79
  62.1 1.9 copy-start.25
  62.2 2.2 copy-start.27
  62.2 2.2 copy-start.28
  63.2 414.6 %all-gather.6.cloned.1.call-start = ((), (), s32[]{:S(2)}) async-start(), calls=%async_computation.3 | async-start | bytes 6684672 | tf_op jit(solution)/shard_map/all_gather | solution.py:138
  64.0 562.3 %all-gather.8.cloned.1.call-start = ((), (), s32[]{:S(2)}) async-start(), calls=%async_computation.4 | async-start | bytes 6684672 | tf_op jit(solution)/shard_map/all_gather | solution.py:141
  353.0 6.4 copy-start.2
  353.0 3.1 copy-start.7
  357.2 2.1 copy-start.3
  357.3 3.1 copy-start.15
  371.1 2.1 copy-start.4
  371.1 3.1 copy-start.16
  375.5 107.6 %copy-start.13 = (f32[128,512]{1,0:T(8,128)}, f32[128,512]{1,0:T(8,128)S(1)}, u32[]{:S(2)}) copy-start(f32[128,512]{1,0:T(8,128)S(1)} %copy.236) | copy-start | bytes 786436
  377.1 504.5 %all-reduce.2.cloned.1.call-start = ((), (), s32[]{:S(2)}) async-start(), calls=%async_computation.5 | async-start | bytes 786432 | tf_op jit(solution)/shard_map/psum | solution.py:200
  491.1 6.2 copy-start.12
  493.6 4.5 copy-start.8
  498.1 5.0 copy-start.26
  503.1 5.7 copy-start.6
  508.8 69.5 %copy-start.14 = (f32[128,512]{1,0:T(8,128)S(1)}, f32[128,512]{1,0:T(8,128)}, u32[]{:S(2)}) copy-start(f32[128,512]{1,0:T(8,128)} %copy-done.13) | copy-start | bytes 786436
  514.3 66.4 %copy-start.11 = (bf16[2048,512]{0,1:T(8,128)(2,1)S(1)}, bf16[2048,512]{0,1:T(8,128)(2,1)}, u32[]{:S(2)}) copy-start(bf16[2048,512]{0,1:T(8,128)(2,1)} %copy.246) | copy-start | bytes 6291460
  577.0 3.6 copy-start.21
  580.7 5.2 copy-start.10
  580.7 5.2 copy-start.22
  580.7 5.2 copy-start.24
  585.9 3.6 copy-start.9
  586.0 3.6 copy-start.23
  634.8 2.9 copy-start.20
  645.6 2.9 copy-start.19
  656.4 3.6 copy-start.18
  660.0 223.4 %copy-start.1 = (bf16[64,1536]{1,0:T(8,128)(2,1)S(1)}, bf16[64,1536]{1,0:T(8,128)(2,1)}, u32[]{:S(2)}) copy-start(bf16[64,1536]{1,0:T(8,128)(2,1)} %param.12) | copy-start | bytes 589828
  (2 other events, 2.8 us)
Sparse Core Ops, SparseCore 0:
  63.3 269.7 all-gather.3
  334.9 142.8 all-gather.5
  480.2 146.0 all-gather.7
  631.7 249.9 all-reduce.1
where the time goes:
time: 891 us; the launch traced here: 890 us
  waiting for transfers between devices  642 us (72%)
  blocking collectives  76.3 us (9%)
  local copies, waits for them, and re-layouts  74.3 us (8%)
  matrix products  71.1 us (8%)
  between operations  14.3 us (2%)
    all_gather x1, waiting for transfers between devices, local(): all_keys = lax.all_gather(key_value, 'blk', axis=0, tiled=True)  267 us
    psum x1, waiting for transfers between devices, local(): gate_grad = lax.psum(gate_term, ('dp', 'blk'))  213 us
    all_gather x1, waiting for transfers between devices, local(): lax.all_gather(queries.astype(jnp.float32), 'blk', axis=0, tiled=True)  98.3 us
    all_gather x1, waiting for transfers between devices, local(): lax.all_gather(grad_out.astype(jnp.float32), 'blk', axis=0, tiled=True)  33.1 us
    all_gather x1, blocking collectives, local(): delta_block = lax.all_gather(row_delta, 'blk', axis=0, tiled=True)  30.8 us
    all_to_all x1, waiting for transfers between devices, local(): lax.all_to_all(rows_in, 'dp', split_axis=2, concat_axis=0, tiled=True)  30.4 us
    all_gather x1, blocking collectives, local(): total_block = lax.all_gather(log_totals.T, 'blk', axis=0, tiled=True)  30 us
    unnamed x67, local copies, waits for them, and re-layouts  24.7 us
  transfers between devices with their start and end apart: 5, of which 5 were waited for; matrix products, arithmetic and copies ran while one was open for 16% of the time, Pallas kernels for 0%

commit v1 on v0

v1 whole, which is shorter than its diff:
```python
import math

import jax
import jax.numpy as jnp
from jax import lax
from jax.experimental import pallas as pl
from jax.experimental.pallas import tpu as pltpu
from jax.sharding import PartitionSpec as P

MESH = pl.DeviceIdType.MESH
HEAD = 128
HEADS = 12
WIDTH = HEADS * HEAD
TOK = 128
SEQ = 2048
FRAME = 128
CLIPS = 4
STEPS = 64
CAP = 16
N_DP = 16
N_BLK = 16
N_Z = 8
CHUNKS = 6
SPAN = 3 * HEAD
ROWS = 256
SLOTS = N_DP * CAP
SCALE = 1.0 / math.sqrt(HEAD)
SCALE2 = SCALE * math.log2(math.e)
NEGATIVE = -1e30
ORDER = ((3, 5, 2, 6, 1, 7), (4, 3, 2, 6, 7, 0), (4, 3, 5, 1, 7, 0), (4, 5, 2, 6, 1, 0))


def skip_of(core, x_lo):
    return 3 - 2 * core - x_lo


def order_at(z, skip, k):
    u = lax.rem(skip - z + 8, 4)
    last = jnp.where(u == 2, ORDER[2][k], ORDER[3][k])
    return jnp.where(u == 0, ORDER[0][k], jnp.where(u == 1, ORDER[1][k], last))


def rank_of(z, skip):
    part = lax.rem(z, 4)
    return (z // 4) * 3 + part - jnp.where(part > skip, 1, 0)


def z_of_rank(rank, skip):
    part = lax.rem(rank, 3)
    return (rank // 3) * 4 + part + jnp.where(part >= skip, 1, 0)


def dot(a, b, dims):
    return lax.dot_general(a, b, (dims, ((), ())), preferred_element_type=jnp.float32)


def wait_for(ref, sem):
    pltpu.make_async_copy(ref, ref, sem).wait()


def kernel(
    rows_ref, slot_ref, clip_ref, reach_ref, step_ref, gate_ref, grad_ref,
    att_ref, qkvg_ref, gg_ref,
    stage, recv, slot_src, slot_dst, bsend, qkv, og, weights, dscore, q_t, do_t, cbuf,
    gacc, gpart, g1, g2,
    a_send, a_recv, sl_send, sl_recv, do_send, do_recv, b_send, b_recv, c_send, ca_recv, cq_recv,
    g1s, g1r, g2s, g2r, g3s, g3r,
):
    dp = lax.axis_index("dp")
    blk = lax.axis_index("blk")
    far_x = dp // 8
    y = lax.rem(dp // 2, 4)
    core = lax.rem(dp, 2)
    z = blk // 2
    x_lo = lax.rem(blk, 2)
    skip = skip_of(core, x_lo)
    is_host = lax.rem(z, 4) != skip
    rank = rank_of(z, skip)
    head = x_lo * CHUNKS + rank
    other_core = 1 - core
    other_z = z_of_rank(rank, skip_of(other_core, x_lo))
    other_blk = other_z * 2 + x_lo

    def remote(src, dst, send, arrive, dp_to, blk_to):
        return pltpu.make_async_remote_copy(
            src_ref=src, dst_ref=dst, send_sem=send, recv_sem=arrive,
            device_id=(dp_to, blk_to), device_id_type=MESH,
        )

    barrier = pltpu.get_barrier_semaphore()

    def greet(dp_to, blk_to):
        pl.semaphore_signal(barrier, inc=1, device_id=(dp_to, blk_to), device_id_type=MESH)

    def greet_plane(n, carry):
        greet(lax.rem(dp + n // 2, N_DP), z * 2 + lax.rem(x_lo + n, 2))
        return carry

    def greet_column(n, carry):
        greet(dp, lax.rem(blk + n, N_BLK))
        return carry

    lax.fori_loop(1, 2 * N_DP, greet_plane, 0)
    lax.fori_loop(1, N_BLK, greet_column, 0)

    @pl.when(is_host)
    def _():
        def greet_other(n, carry):
            greet(2 * n + other_core, other_blk)
            return carry

        lax.fori_loop(0, N_DP // 2, greet_other, 0)

    own = core * 8 + dp // 2

    def stage_base(k, x_to, core_to):
        return ((k * 2 + x_to) * 2 + core_to) * 128

    for core_to in (0, 1):
        for k in range(CHUNKS):
            for x_to in (0, 1):
                far = skip_of(core_to, x_to)
                z_to = lax.rem(z + order_at(z, far, k), N_Z)
                column = pl.multiple_of((x_to * CHUNKS + rank_of(z_to, far)) * HEAD, HEAD)
                base = stage_base(k, x_to, core_to)
                for part in range(3):
                    stage[base : base + 128, part * HEAD : (part + 1) * HEAD] = rows_ref[
                        :, core_to, :, pl.ds(part * WIDTH + column, HEAD)
                    ].reshape(128, HEAD)

    lane = lax.broadcasted_iota(jnp.int32, (CAP, SLOTS), 1)
    spread = (lane == lax.broadcasted_iota(jnp.int32, (CAP, SLOTS), 0) + dp * CAP).astype(jnp.bfloat16)
    slots = dot(slot_ref[...].astype(jnp.bfloat16), spread, ((1,), (0,)))
    for q in range(N_DP):
        slot_src[q] = slots[q : q + 1, :]
    source = x_lo * N_DP + dp
    slot_dst[pl.ds(source, 1)] = slot_src[pl.ds(dp, 1)]
    for k in range(CHUNKS):
        recv[pl.ds(pl.multiple_of(k * 512 + source * CAP, CAP), CAP), :] = stage[
            pl.ds(pl.multiple_of(((k * 2 + x_lo) * 16 + own) * CAP, CAP), CAP), :
        ]

    @pl.when(is_host)
    def _():
        og[pl.ds(pl.multiple_of(blk * TOK, TOK), TOK), :] = grad_ref[
            :, pl.ds(pl.multiple_of(head * HEAD, HEAD), HEAD)
        ]
        pl.semaphore_wait(barrier, 2 * N_DP - 1 + N_BLK - 1 + N_DP // 2)

    @pl.when(jnp.logical_not(is_host))
    def _():
        pl.semaphore_wait(barrier, 2 * N_DP - 1 + N_BLK - 1)

    def send_slots(n, carry):
        dp_to = lax.rem(dp + n // 2, N_DP)
        remote(
            slot_src.at[dp_to], slot_dst.at[source], sl_send, sl_recv, dp_to, z * 2 + lax.rem(x_lo + n, 2)
        ).start()
        return carry

    lax.fori_loop(1, 2 * N_DP, send_slots, 0)

    for core_to in (0, 1):
        for k in range(CHUNKS):
            def send_rows(n, carry, core_to=core_to, k=k):
                half = lax.rem(far_x + n // 8, 2) * 4 + lax.rem(y + lax.rem(n // 2, 4), 4)
                x_to = lax.rem(x_lo + n, 2)
                src = ((k * 2 + x_to) * 16 + core_to * 8 + half) * CAP
                remote(
                    stage.at[pl.ds(pl.multiple_of(src, CAP), CAP), :],
                    recv.at[pl.ds(pl.multiple_of(k * 512 + source * CAP, CAP), CAP), :],
                    a_send, a_recv.at[k], half * 2 + core_to, z * 2 + x_to,
                ).start()
                return carry

            lax.fori_loop(1, 16, send_rows, 0)

            @pl.when(core != core_to)
            def _():
                send_rows(0, 0)

            if core_to == 0:
                for x_to in (0, 1):
                    far = skip_of(core, x_to)
                    z_to = lax.rem(z + order_at(z, far, k), N_Z)
                    column = (x_to * CHUNKS + rank_of(z_to, far)) * HEAD
                    blk_to = z_to * 2 + x_to

                    @pl.when(blk_to != blk)
                    def _():
                        remote(
                            grad_ref.at[:, pl.ds(pl.multiple_of(column, HEAD), HEAD)],
                            og.at[pl.ds(pl.multiple_of(blk * TOK, TOK), TOK), :],
                            do_send, do_recv, dp, blk_to,
                        ).start()

    ids = clip_ref[...]
    ends = []
    for c in range(CLIPS):
        ends.append(
            jnp.sum(jnp.where(ids <= c, 1.0, 0.0), axis=1, keepdims=True).astype(jnp.int32)
        )
    starts = [jnp.zeros((1, 1), jnp.int32)] + ends[:-1]

    wait_for(slot_dst.at[pl.ds(0, 31)], sl_recv)
    row_of = lax.broadcasted_iota(jnp.int32, (TOK, SLOTS), 0).astype(jnp.float32)
    placing = []
    for half in range(2):
        slot_row = jnp.sum(slot_dst[half * N_DP : (half + 1) * N_DP], axis=0)
        placing.append(jnp.where(row_of == slot_row, 1.0, 0.0).astype(jnp.bfloat16))
    here = pl.ds(pl.multiple_of(z * ROWS, ROWS), ROWS)
    for k in range(CHUNKS):
        wait_for(recv.at[pl.ds(k * 512, 31 * CAP), :], a_recv.at[k])
        z_to = lax.rem(z + order_at(z, skip, k), N_Z)
        for half in range(2):
            low = k * 512 + half * SLOTS
            bsend[k * ROWS + half * TOK : k * ROWS + (half + 1) * TOK, :] = dot(
                placing[half], recv[low : low + SLOTS, :], ((1,), (0,))
            ).astype(jnp.bfloat16)
        piece = pl.ds(k * ROWS, ROWS)

        @pl.when(z_to != z)
        def _():
            remote(bsend.at[piece, :], qkv.at[here, :], b_send, b_recv, dp, z_to * 2 + x_lo).start()

        @pl.when(z_to == z)
        def _():
            qkv[here, :] = bsend[piece, :]

    @pl.when(is_host)
    def _():
        wait_for(og.at[pl.ds(0, 15 * TOK), :], do_recv)
        wait_for(qkv.at[pl.ds(0, 7 * ROWS), :], b_recv)
        gacc[...] = jnp.zeros((8, HEAD), jnp.float32)
        head_gate = gate_ref[:, pl.ds(pl.multiple_of(head * HEAD, HEAD), HEAD)]

        def send_back(which, z_to, target, column):
            for half in range(2):
                blk_to = z_to * 2 + half
                block = cbuf.at[
                    pl.ds(pl.multiple_of(which * SEQ + z_to * ROWS + half * TOK, TOK), TOK), :
                ]
                place = target.at[:, pl.ds(pl.multiple_of(column * WIDTH + head * HEAD, HEAD), HEAD)]

                @pl.when(blk_to != blk)
                def _():
                    arrive = ca_recv if which == 0 else cq_recv
                    remote(block, place, c_send, arrive, dp, blk_to).start()

                @pl.when(blk_to == blk)
                def _():
                    place[...] = block[...]

        def row_block(n, carry):
            z_to = lax.rem(z + 4 + n, N_Z)
            base = pl.multiple_of(z_to * ROWS, ROWS)
            rows = pl.ds(base, ROWS)
            index = lax.broadcasted_iota(jnp.int32, (ROWS, 1), 0) + base
            low = jnp.zeros((ROWS, 1), jnp.int32)
            high = jnp.zeros((ROWS, 1), jnp.int32)
            step = jnp.zeros((ROWS, 1), jnp.int32)
            inside = []
            for c in range(CLIPS):
                member = (index >= starts[c]) & (index < ends[c])
                inside.append(member)
                stop = starts[c] + ((index - starts[c]) // FRAME + 1 + reach_ref[0, c]) * FRAME
                low = jnp.where(member, starts[c], low)
                high = jnp.where(member, jnp.minimum(stop, ends[c]), high)
                step = jnp.where(member, step_ref[0, c], step)
            queries = qkv[rows, 0:HEAD]
            scores = dot(queries, qkv[:, HEAD : 2 * HEAD], ((1,), (1,)))
            column = lax.broadcasted_iota(jnp.int32, (ROWS, SEQ), 1)
            scores = jnp.where((column >= low) & (column < high), scores, NEGATIVE)
            top = jnp.max(scores, axis=1, keepdims=True)
            parts = jnp.exp2((scores - top) * SCALE2)
            inverse = 1.0 / jnp.sum(parts, axis=1, keepdims=True)
            parts = parts.astype(jnp.bfloat16)
            weights[rows, :] = parts
            attention = dot(parts, qkv[:, 2 * HEAD : 3 * HEAD], ((1,), (0,))) * inverse
            hot = (step == lax.broadcasted_iota(jnp.int32, (ROWS, STEPS), 1)).astype(jnp.bfloat16)
            gate_rows = dot(hot, head_gate, ((1,), (0,)))
            grad = og[rows, :].astype(jnp.float32)
            grad_out = (gate_rows * grad).astype(jnp.bfloat16).astype(jnp.float32)
            cbuf[rows, :] = (gate_rows * attention).astype(jnp.bfloat16)
            send_back(0, z_to, att_ref, 0)
            delta = jnp.sum(grad_out * attention, axis=1, keepdims=True) * inverse
            grad_out = grad_out * inverse
            do_t[:, rows] = grad_out.T.astype(jnp.bfloat16)
            q_t[:, rows] = queries.astype(jnp.float32).T.astype(jnp.bfloat16)
            prob_grad = dot(grad_out.astype(jnp.bfloat16), qkv[:, 2 * HEAD : 3 * HEAD], ((1,), (1,)))
            score_grad = (weights[rows, :].astype(jnp.float32) * (prob_grad - delta)).astype(jnp.bfloat16)
            dscore[rows, :] = score_grad
            query_grad = dot(score_grad, qkv[:, HEAD : 2 * HEAD], ((1,), (0,))) * SCALE
            cbuf[pl.ds(pl.multiple_of(SEQ + base, ROWS), ROWS), :] = query_grad.astype(jnp.bfloat16)
            send_back(1, z_to, qkvg_ref, 0)
            product = grad * attention
            for c in range(CLIPS):
                gacc[c : c + 1, :] += jnp.sum(jnp.where(inside[c], product, 0.0), axis=0, keepdims=True)
            return carry

        lax.fori_loop(0, N_Z, row_block, 0)

        step_row = lax.broadcasted_iota(jnp.int32, (STEPS, HEAD), 0)
        total = jnp.zeros((STEPS, HEAD), jnp.float32)
        for c in range(CLIPS):
            total = total + jnp.where(step_row == step_ref[0, c], gacc[c : c + 1, :], 0.0)
        for p in range(N_DP):
            gpart[p] = total[4 * p : 4 * p + 4, :]
        g1[pl.ds(dp, 1)] = gpart[pl.ds(dp, 1)]

        def send_gate(n, carry):
            dp_to = lax.rem(dp + n, N_DP)
            blk_to = jnp.where(lax.rem(dp_to, 2) == core, blk, other_blk)
            remote(gpart.at[dp_to], g1.at[dp], g1s, g1r, dp_to, blk_to).start()
            return carry

        lax.fori_loop(1, N_DP, send_gate, 0)

        def column_block(n, carry):
            z_to = lax.rem(z + 4 + n, N_Z)
            base = pl.multiple_of(z_to * ROWS, ROWS)
            columns = pl.ds(base, ROWS)
            key_grad = dot(q_t[...], dscore[:, columns], ((1,), (0,))) * SCALE
            cbuf[pl.ds(pl.multiple_of(2 * SEQ + base, ROWS), ROWS), :] = key_grad.T.astype(jnp.bfloat16)
            send_back(2, z_to, qkvg_ref, 1)
            value_grad = dot(do_t[...], weights[:, columns], ((1,), (0,)))
            cbuf[pl.ds(pl.multiple_of(3 * SEQ + base, ROWS), ROWS), :] = value_grad.T.astype(jnp.bfloat16)
            send_back(3, z_to, qkvg_ref, 2)
            return carry

        lax.fori_loop(0, N_Z, column_block, 0)

        wait_for(g1.at[pl.ds(0, 15)], g1r)
        g2[dp, head] = jnp.sum(g1[...], axis=0)

        def send_sum(n, carry):
            mine = g2.at[dp, head]
            remote(mine, mine, g2s, g2r, dp, lax.rem(blk + n, N_BLK)).start()
            return carry

        lax.fori_loop(1, N_BLK, send_sum, 0)
        wait_for(g2.at[dp, pl.ds(0, 11)], g2r)

    @pl.when(jnp.logical_not(is_host))
    def _():
        wait_for(g2.at[dp], g2r)

    def send_steps(n, carry):
        mine = g2.at[dp]
        remote(mine, mine, g3s, g3r, lax.rem(dp + n, N_DP), blk).start()
        return carry

    lax.fori_loop(1, N_DP, send_steps, 0)

    wait_for(slot_dst.at[pl.ds(0, 31)], sl_send)
    wait_for(stage.at[pl.ds(0, 186 * CAP), :], a_send)
    wait_for(g2.at[pl.ds(0, 15)], g3r)
    for p in range(N_DP):
        for h in range(HEADS):
            gg_ref[4 * p : 4 * p + 4, h * HEAD : (h + 1) * HEAD] = g2[p, h]

    @pl.when(is_host)
    def _():
        wait_for(grad_ref.at[:, pl.ds(0, 11 * HEAD)], do_send)
        wait_for(bsend.at[pl.ds(0, 5 * ROWS), :], b_send)
        wait_for(gpart.at[pl.ds(0, 15)], g1s)
        wait_for(gpart.at[pl.ds(0, 15)], g2s)
        wait_for(att_ref.at[:, pl.ds(0, 11 * HEAD)], ca_recv)
        wait_for(qkvg_ref.at[:, pl.ds(0, 33 * HEAD)], cq_recv)
        wait_for(cbuf.at[pl.ds(0, 60 * TOK), :], c_send)

    @pl.when(jnp.logical_not(is_host))
    def _():
        wait_for(grad_ref, do_send)
        wait_for(bsend, b_send)
        wait_for(att_ref, ca_recv)
        wait_for(qkvg_ref, cq_recv)

    wait_for(g2.at[pl.ds(0, 15)], g3s)


def local(rows_in, slot_rows, clip_ids, clip_reach, clip_step, gate_table, out_grad):
    vmem = pl.BlockSpec(memory_space=pltpu.VMEM)
    smem = pl.BlockSpec(memory_space=pltpu.SMEM)
    bf16, f32 = jnp.bfloat16, jnp.float32
    sem = pltpu.SemaphoreType.DMA
    attended, qkv_grad, gate_grad = pl.pallas_call(
        kernel,
        out_shape=(
            jax.ShapeDtypeStruct((TOK, WIDTH), bf16),
            jax.ShapeDtypeStruct((TOK, 3 * WIDTH), bf16),
            jax.ShapeDtypeStruct((STEPS, WIDTH), f32),
        ),
        in_specs=[vmem, vmem, vmem, smem, smem, vmem, vmem],
        out_specs=(vmem, vmem, vmem),
        scratch_shapes=[
            pltpu.VMEM((CHUNKS * 2 * N_DP * CAP, SPAN), bf16),
            pltpu.VMEM((CHUNKS * 2 * SLOTS, SPAN), bf16),
            pltpu.VMEM((N_DP, 1, SLOTS), f32),
            pltpu.VMEM((2 * N_DP, 1, SLOTS), f32),
            pltpu.VMEM((CHUNKS * ROWS, SPAN), bf16),
            pltpu.VMEM((SEQ, SPAN), bf16),
            pltpu.VMEM((SEQ, HEAD), bf16),
            pltpu.VMEM((SEQ, SEQ), bf16),
            pltpu.VMEM((SEQ, SEQ), bf16),
            pltpu.VMEM((HEAD, SEQ), bf16),
            pltpu.VMEM((HEAD, SEQ), bf16),
            pltpu.VMEM((4 * SEQ, HEAD), bf16),
            pltpu.VMEM((8, HEAD), f32),
            pltpu.VMEM((N_DP, 4, HEAD), f32),
            pltpu.VMEM((N_DP, 4, HEAD), f32),
            pltpu.VMEM((N_DP, HEADS, 4, HEAD), f32),
            sem, sem((CHUNKS,)), sem, sem, sem, sem, sem, sem, sem, sem, sem,
            sem, sem, sem, sem, sem, sem,
        ],
        compiler_params=pltpu.CompilerParams(
            collective_id=0, has_side_effects=True, vmem_limit_bytes=56 * 2**20
        ),
        name="attention",
    )(
        rows_in.reshape(8, 2, CAP, 3 * WIDTH),
        slot_rows.reshape(N_DP, CAP),
        clip_ids,
        clip_reach,
        clip_step,
        gate_table,
        out_grad[0],
    )
    return attended[None], qkv_grad[None], gate_grad


def solution(mesh):
    return jax.shard_map(
        local,
        mesh=mesh,
        in_specs=(
            P("dp", "blk", None, None, None),
            P("dp", "blk", None, None),
            P("dp", None),
            P("dp", None),
            P("dp", None),
            P(),
            P("dp", "blk", None),
        ),
        out_specs=(P("dp", "blk", None), P("dp", "blk", None), P()),
        check_vma=False,
    )
```

time: 891 us -> 123 us (0.14)
  waiting for transfers between devices: 642 us -> 0 us
  Pallas kernels: 0 us -> 118 us
  blocking collectives: 76.3 us -> 0 us
  matrix products: 71.1 us -> 0 us
  local copies, waits for them, and re-layouts: 74.3 us -> 4.93 us
  between operations: 14.3 us -> 0.64 us
    all_gather x3 -> x0, waiting for transfers between devices: 399 us -> none  [the longest x1 267 us: local(): all_keys = lax.all_gather(key_value, 'blk', axis=0, tiled=True)]
    psum x1 -> x0, waiting for transfers between devices: 213 us -> none  [local(): gate_grad = lax.psum(gate_term, ('dp', 'blk'))]
    pallas_call x0 -> x1, Pallas kernels: none -> 118 us  [local(): pl.pallas_call(kernel, out_shape=(jax.ShapeDtypeStruct((TOK, WIDTH), bf16...]
    dot_general x21 -> x0, matrix products: 71.1 us -> none  [the longest x3 15.9 us: local(): jnp.einsum('hrk,khd->rhd', score_grad, keys_group, preferred_element_type...]
    all_gather x2 -> x0, blocking collectives: 60.8 us -> none  [the longest x1 30.8 us: local(): delta_block = lax.all_gather(row_delta, 'blk', axis=0, tiled=True)]
    all_to_all x1 -> x0, waiting for transfers between devices: 30.4 us -> none  [local(): lax.all_to_all(rows_in, 'dp', split_axis=2, concat_axis=0, tiled=True)]
    reshape x12 -> x0, local copies, waits for them, and re-layouts: 30.1 us -> none  [the longest x3 10.5 us: local(): query_block[:, column_low:column_low + group_span]]
    unnamed x67 -> x5, local copies, waits for them, and re-layouts: 24.7 us -> 4.93 us
  transfers between devices with their start and end apart: 5 -> 0, of which waited for: 5 -> 0; matrix products, arithmetic and copies ran while one was open for 16% -> 0% of each run, Pallas kernels for 0% -> 0%
where the time goes in v1:
time: 123 us
  Pallas kernels  118 us (96%)
  local copies, waits for them, and re-layouts  4.93 us (4%)
    pallas_call x1, Pallas kernels, local(): pl.pallas_call(kernel, out_shape=(jax.ShapeDtypeStruct((TOK, WIDTH), bf16...  118 us
    unnamed x5, local copies, waits for them, and re-layouts  4.93 us

profile of v1, /device:TPU:1, one launch (start us, length us, event | category | flops | bytes accessed | tf_op | source)
XLA Modules:
  0.0 123.3 jit_solution(6326681012029395272)
XLA Ops:
  0.6 117.7 %attention.1 = (bf16[128,1536]{1,0:T(8,128)(2,1)}, bf16[128,4608]{1,0:T(8,128)(2,1)}, f32[64,1536]{1,0:T(8,128)}) custom-call(bf16[8,2,16,4608]{3,2,1,0:T(8,128)(2,1)} %bitcast.5, s32[16,16]{1,0:T(8,128)} %bitcast.9, s32[1,2048]{1,0:T(1,128)} %clip_ref.1, s32[1,4]{1,0:T(1,128)} %reach_ref.1, s32[1,4]{1,0:T(1,128)} %step_ref.1, bf16[64,1536]{1,0:T(8,128)(2,1)} %gate_ref.1, ...), custom_call_target="tpu_custom_call" | custom-call | tf_op jit(solution)/shard_map/attention/pallas_call | solution.py:387
  118.3 1.8 %copy.13 = bf16[1,128,1536]{2,1,0:T(8,128)(2,1)} copy(bf16[1,128,1536]{2,1,0:T(8,128)(2,1)} %bitcast.7) | data formatting | bytes 786432
  120.1 0.0 copy-start
  120.1 2.4 %copy.14 = bf16[1,128,4608]{2,1,0:T(8,128)(2,1)} copy(bf16[1,128,4608]{2,1,0:T(8,128)(2,1)} %bitcast.6) | data formatting | bytes 2359296
  122.5 0.0 copy-done
  122.5 0.7 copy.15
Async XLA Ops:
  120.1 2.4 %copy-start = (f32[64,1536]{1,0:T(8,128)S(1)}, f32[64,1536]{1,0:T(8,128)}, u32[]{:S(2)}) copy-start(f32[64,1536]{1,0:T(8,128)} %get-tuple-element.14) | copy-start | bytes 1179652

commit v2 on v1

v2 whole, which is shorter than its diff:
```python
import math

import jax
import jax.numpy as jnp
from jax import lax
from jax.experimental import pallas as pl
from jax.experimental.pallas import tpu as pltpu
from jax.sharding import PartitionSpec as P

MESH = pl.DeviceIdType.MESH
HEAD = 128
HEADS = 12
WIDTH = HEADS * HEAD
TOK = 128
SEQ = 2048
FRAME = 128
CLIPS = 4
STEPS = 64
CAP = 16
N_DP = 16
N_BLK = 16
N_Z = 8
CHUNKS = 6
SPAN = 3 * HEAD
ROWS = 256
TILE = 512
SLOTS = N_DP * CAP
SCALE = 1.0 / math.sqrt(HEAD)
SCALE2 = SCALE * math.log2(math.e)
NEGATIVE = -1e30
Q0, K0, U0, V0, ONE0 = 0, 128, 256, 384, 512
RETURNS = (4, 3, 5, 2, 6, 1, 7, 0)
ORDER = ((3, 5, 2, 6, 1, 7), (4, 3, 2, 6, 7, 0), (4, 3, 5, 1, 7, 0), (4, 5, 2, 6, 1, 0))


def skip_of(core, x_lo):
    return 3 - 2 * core - x_lo


def order_at(z, skip, k):
    u = lax.rem(skip - z + 8, 4)
    last = jnp.where(u == 2, ORDER[2][k], ORDER[3][k])
    return jnp.where(u == 0, ORDER[0][k], jnp.where(u == 1, ORDER[1][k], last))


def rank_of(z, skip):
    part = lax.rem(z, 4)
    return (z // 4) * 3 + part - jnp.where(part > skip, 1, 0)


def z_of_rank(rank, skip):
    part = lax.rem(rank, 3)
    return (rank // 3) * 4 + part + jnp.where(part >= skip, 1, 0)


def dot(a, b, dims):
    return lax.dot_general(a, b, (dims, ((), ())), preferred_element_type=jnp.float32)


def wait_for(ref, sem):
    pltpu.make_async_copy(ref, ref, sem).wait()


def kernel(
    rows_ref, slot_ref, clip_ref, reach_ref, step_ref, gate_ref, grad_ref,
    att_ref, qkvg_ref, gg_ref,
    stage, recv, slot_src, slot_dst, bsend, wide, og, units, gates, grads, grads_up, step_hot,
    weights, dscore, scores_a, scores_b, q_t, do_t, cbuf, gpart, g1, g2,
    a_send, a_recv, sl_send, sl_recv, do_send, do_recv, b_send, b_recv, c_send, ca_recv, cq_recv,
    g1s, g1r, g2s, g2r, g3s, g3r, go,
):
    dp = lax.axis_index("dp")
    blk = lax.axis_index("blk")
    far_x = dp // 8
    y = lax.rem(dp // 2, 4)
    core = lax.rem(dp, 2)
    z = blk // 2
    x_lo = lax.rem(blk, 2)
    skip = skip_of(core, x_lo)
    is_host = lax.rem(z, 4) != skip
    rank = rank_of(z, skip)
    head = x_lo * CHUNKS + rank
    other_core = 1 - core
    other_z = z_of_rank(rank, skip_of(other_core, x_lo))
    other_blk = other_z * 2 + x_lo

    def remote(src, dst, send, arrive, dp_to, blk_to):
        return pltpu.make_async_remote_copy(
            src_ref=src, dst_ref=dst, send_sem=send, recv_sem=arrive,
            device_id=(dp_to, blk_to), device_id_type=MESH,
        )

    barrier = pltpu.get_barrier_semaphore()

    def greet(dp_to, blk_to):
        pl.semaphore_signal(barrier, inc=1, device_id=(dp_to, blk_to), device_id_type=MESH)

    halves = []
    for n in range(8):
        halves.append(lax.rem(far_x + n // 4, 2) * 4 + lax.rem(y + n % 4, 4))
    x_tos = (x_lo, 1 - x_lo)
    blk_tos = (z * 2 + x_lo, z * 2 + 1 - x_lo)
    plane = [(n, 0) for n in range(1, 16)] + [(n, 1) for n in range(16)]
    cores = (core, 1 - core)
    for n, other in plane:
        greet(halves[n // 2] * 2 + cores[other], blk_tos[n % 2])
    for n in range(1, N_BLK):
        greet(dp, lax.rem(blk + n, N_BLK))

    @pl.when(is_host)
    def _():
        for n in range(8):
            greet(halves[n] * 2 + other_core, other_blk)

    own = core * 8 + dp // 2

    def stage_base(k, x_to, core_to):
        return ((k * 2 + x_to) * 2 + core_to) * 128

    for core_to in (0, 1):
        for k in range(CHUNKS):
            for x_to in (0, 1):
                far = skip_of(core_to, x_to)
                z_to = lax.rem(z + order_at(z, far, k), N_Z)
                column = pl.multiple_of((x_to * CHUNKS + rank_of(z_to, far)) * HEAD, HEAD)
                base = stage_base(k, x_to, core_to)
                for part in range(3):
                    stage[base : base + 128, part * HEAD : (part + 1) * HEAD] = rows_ref[
                        :, core_to, :, pl.ds(part * WIDTH + column, HEAD)
                    ].reshape(128, HEAD)

    lane = lax.broadcasted_iota(jnp.int32, (CAP, SLOTS), 1)
    spread = (lane == lax.broadcasted_iota(jnp.int32, (CAP, SLOTS), 0) + dp * CAP).astype(jnp.bfloat16)
    slots = dot(slot_ref[...].astype(jnp.bfloat16), spread, ((1,), (0,)))
    for q in range(N_DP):
        slot_src[q] = slots[q : q + 1, :]
    source = x_lo * N_DP + dp
    slot_dst[pl.ds(source, 1)] = slot_src[pl.ds(dp, 1)]
    for k in range(CHUNKS):
        recv[pl.ds(pl.multiple_of(k * 512 + source * CAP, CAP), CAP), :] = stage[
            pl.ds(pl.multiple_of(((k * 2 + x_lo) * 16 + own) * CAP, CAP), CAP), :
        ]

    @pl.when(is_host)
    def _():
        og[pl.ds(pl.multiple_of(blk * TOK, TOK), TOK), :] = grad_ref[
            :, pl.ds(pl.multiple_of(head * HEAD, HEAD), HEAD)
        ]
        pl.semaphore_wait(barrier, 2 * N_DP - 1 + N_BLK - 1 + N_DP // 2)

    @pl.when(jnp.logical_not(is_host))
    def _():
        pl.semaphore_wait(barrier, 2 * N_DP - 1 + N_BLK - 1)

    for n, other in plane:
        dp_to = halves[n // 2] * 2 + cores[other]
        remote(slot_src.at[dp_to], slot_dst.at[source], sl_send, sl_recv, dp_to, blk_tos[n % 2]).start()

    source_row = source * CAP
    targets = [x_tos[n % 2] * 256 + halves[n // 2] * CAP for n in range(16)]

    for core_to in (0, 1):
        for k in range(CHUNKS):
            for n in range(16):
                copy = remote(
                    stage.at[pl.ds(pl.multiple_of(targets[n] + (k * 512 + core_to * 128), CAP), CAP), :],
                    recv.at[pl.ds(pl.multiple_of(source_row + k * 512, CAP), CAP), :],
                    a_send, a_recv.at[k], halves[n // 2] * 2 + core_to, blk_tos[n % 2],
                )
                if n:
                    copy.start()
                else:
                    pl.when(core != core_to)(copy.start)

            if core_to == 0:
                for x_to in (0, 1):
                    far = skip_of(core, x_to)
                    z_to = lax.rem(z + order_at(z, far, k), N_Z)
                    column = (x_to * CHUNKS + rank_of(z_to, far)) * HEAD
                    blk_to = z_to * 2 + x_to

                    @pl.when(blk_to != blk)
                    def _():
                        remote(
                            grad_ref.at[:, pl.ds(pl.multiple_of(column, HEAD), HEAD)],
                            og.at[pl.ds(pl.multiple_of(blk * TOK, TOK), TOK), :],
                            do_send, do_recv, dp, blk_to,
                        ).start()

    ids = clip_ref[...]
    ends = []
    for c in range(CLIPS):
        ends.append(
            jnp.sum(jnp.where(ids <= c, 1.0, 0.0), axis=1, keepdims=True).astype(jnp.int32)
        )
    starts = [jnp.zeros((1, 1), jnp.int32)] + ends[:-1]

    @pl.when(is_host)
    def _():
        head_gate = gate_ref[:, pl.ds(pl.multiple_of(head * HEAD, HEAD), HEAD)]
        unit = lax.broadcasted_iota(jnp.int32, (1, HEAD), 1)
        key_low = jnp.full((1, HEAD), SEQ, jnp.int32)
        key_high = jnp.full((1, HEAD), SEQ, jnp.int32)
        row_low = jnp.full((1, HEAD), SEQ, jnp.int32)
        row_high = jnp.full((1, HEAD), SEQ, jnp.int32)
        step_lane = jnp.zeros((1, SEQ), jnp.int32)
        step_of = lax.broadcasted_iota(jnp.int32, (STEPS, HEAD), 0)
        clip_gates = []
        first = jnp.zeros((1, 1), jnp.int32)
        for c in range(CLIPS):
            last = first + (ends[c] - starts[c] + FRAME - 1) // FRAME
            member = (unit >= first) & (unit < last)
            block = unit - first
            key_low = jnp.where(member, starts[c] + block * FRAME, key_low)
            key_high = jnp.where(member, jnp.minimum(starts[c] + block * FRAME + FRAME, ends[c]), key_high)
            row_low = jnp.where(member, starts[c] + jnp.maximum(block - reach_ref[0, c], 0) * FRAME, row_low)
            row_high = jnp.where(member, ends[c], row_high)
            first = last
            step_lane = jnp.where(ids == c, step_ref[0, c], step_lane)
            clip_gates.append(
                jnp.sum(
                    jnp.where(step_of == step_ref[0, c], head_gate.astype(jnp.float32), 0.0),
                    axis=0, keepdims=True,
                )
            )
        step_hot[...] = (
            lax.broadcasted_iota(jnp.int32, (STEPS, SEQ), 0) == step_lane
        ).astype(jnp.bfloat16)
        number = lax.broadcasted_iota(jnp.int32, (ROWS, HEAD), 0)

        def layout(n, carry):
            base = pl.multiple_of(n * ROWS, ROWS)
            rows = pl.ds(base, ROWS)
            index = number + base
            wide[rows, U0 : U0 + HEAD] = jnp.where((index >= key_low) & (index < key_high), 1.0, 0.0).astype(jnp.bfloat16)
            wide[rows, ONE0 : ONE0 + HEAD] = jnp.ones((ROWS, HEAD), jnp.bfloat16)
            units[rows, :] = jnp.where((index >= row_low) & (index < row_high), 0.0, NEGATIVE).astype(jnp.bfloat16)
            gate = clip_gates[CLIPS - 1]
            for c in reversed(range(CLIPS - 1)):
                gate = jnp.where(index < ends[c], clip_gates[c], gate)
            gates[rows, :] = gate.astype(jnp.bfloat16)
            return carry

        lax.fori_loop(0, N_Z, layout, 0)

    wait_for(slot_dst.at[pl.ds(0, 31)], sl_recv)
    row_of = lax.broadcasted_iota(jnp.int32, (TOK, SLOTS), 0).astype(jnp.float32)
    placing = []
    for half in range(2):
        slot_row = jnp.sum(slot_dst[half * N_DP : (half + 1) * N_DP], axis=0)
        placing.append(jnp.where(row_of == slot_row, 1.0, 0.0).astype(jnp.bfloat16))
    here = pl.ds(pl.multiple_of(z * ROWS, ROWS), ROWS)
    for k in range(CHUNKS):
        wait_for(recv.at[pl.ds(k * 512, 31 * CAP), :], a_recv.at[k])
        z_to = lax.rem(z + order_at(z, skip, k), N_Z)
        for half in range(2):
            low = k * 512 + half * SLOTS
            bsend[k * ROWS + half * TOK : k * ROWS + (half + 1) * TOK, :] = dot(
                placing[half], recv[low : low + SLOTS, :], ((1,), (0,))
            ).astype(jnp.bfloat16)
        piece = pl.ds(k * ROWS, ROWS)

        @pl.when(z_to != z)
        def _():
            blk_to = z_to * 2 + x_lo
            remote(
                bsend.at[piece, 0 : 2 * HEAD], wide.at[here, Q0:U0], b_send, b_recv, dp, blk_to
            ).start()
            remote(
                bsend.at[piece, 2 * HEAD : SPAN], wide.at[here, V0:ONE0], b_send, b_recv, dp, blk_to
            ).start()

        @pl.when(z_to == z)
        def _():
            wide[here, Q0:U0] = bsend[piece, 0 : 2 * HEAD]
            wide[here, V0:ONE0] = bsend[piece, 2 * HEAD : SPAN]

    def zs_rows(n, which=0):
        base = lax.rem(z + RETURNS[n], N_Z) * ROWS
        return pl.ds(pl.multiple_of(which * SEQ + base, ROWS), ROWS)

    def send_back(which, n):
        target, column, arrive = (
            (att_ref, 0, ca_recv), (qkvg_ref, 0, cq_recv), (qkvg_ref, 1, cq_recv), (qkvg_ref, 2, cq_recv)
        )[which]
        z_to = lax.rem(z + RETURNS[n], N_Z)
        place = target.at[:, pl.ds(pl.multiple_of(column * WIDTH + head * HEAD, HEAD), HEAD)]
        for half in range(2):
            block = cbuf.at[
                pl.ds(pl.multiple_of(which * SEQ + z_to * ROWS + half * TOK, TOK), TOK), :
            ]
            copy = remote(block, place, c_send, arrive, dp, z_to * 2 + half)
            if RETURNS[n]:
                copy.start()
            else:
                pl.when(half != x_lo)(copy.start)

                @pl.when(half == x_lo)
                def _():
                    place[...] = block[...]

    @pl.when(core == 1)
    def _():
        @pl.when(is_host)
        def _():
            wait_for(bsend.at[pl.ds(0, 5 * ROWS), :], b_send)

        @pl.when(jnp.logical_not(is_host))
        def _():
            wait_for(bsend, b_send)

        pl.semaphore_signal(go, inc=1, device_id=(halves[0] * 2, blk), device_id_type=MESH)

    @pl.when(is_host)
    def _():
        wait_for(og.at[pl.ds(0, 15 * TOK), :], do_recv)
        grads[...] = (gates[...].astype(jnp.float32) * og[...].astype(jnp.float32)).astype(jnp.bfloat16)
        wait_for(recv.at[pl.ds(0, 7 * ROWS), :], b_recv)

        scores = (scores_a, scores_b)

        def score_tile(n, t, queries, top):
            keys = wide[t * TILE : (t + 1) * TILE, K0:V0]
            tile = dot(queries, keys, ((1,), (1,)))
            scores[n % 2][:, t * TILE : (t + 1) * TILE] = tile
            for u in range(TILE // HEAD):
                part = tile[:, u * HEAD : (u + 1) * HEAD]
                top = part if top is None else jnp.maximum(top, part)
            return top

        def query_rows(n):
            return jnp.concatenate([wide[zs_rows(n), Q0:K0], units[zs_rows(n), :]], axis=1)

        lane_of = lax.broadcasted_iota(jnp.int32, (ROWS, HEAD), 1)
        step_total = jnp.zeros((STEPS, HEAD), jnp.float32)
        top = None
        queries = query_rows(0)
        for t in range(SEQ // TILE):
            top = score_tile(0, t, queries, top)
        eye = jnp.where(
            lax.broadcasted_iota(jnp.int32, (HEAD, HEAD), 0) == lax.broadcasted_iota(jnp.int32, (HEAD, HEAD), 1), 1.0, 0.0
        ).astype(jnp.bfloat16)

        def split(rest):
            high = rest.astype(jnp.bfloat16)
            rest = rest - high.astype(jnp.float32)
            middle = rest.astype(jnp.bfloat16)
            return high, middle, (rest - middle.astype(jnp.float32)).astype(jnp.bfloat16)

        def finish_rows(n, summed, step_total):
            rows = zs_rows(n)
            inverse = 1.0 / summed[:, HEAD:]
            attention = summed[:, :HEAD] * inverse
            cbuf[zs_rows(n), :] = (gates[rows, :].astype(jnp.float32) * attention).astype(jnp.bfloat16)
            pl.when(core == 1)(lambda: send_back(0, n))
            grad_out = grads[rows, :].astype(jnp.float32)
            row_delta = jnp.sum(grad_out * attention, axis=1, keepdims=True) * inverse
            grad_out = (grad_out * inverse).astype(jnp.bfloat16)
            high, middle, small = split(-row_delta)
            zero = jnp.zeros((ROWS, HEAD), jnp.bfloat16)
            grads_up[rows, 0:HEAD] = grad_out
            grads_up[rows, HEAD:] = jnp.where(
                lane_of == 0, high, jnp.where(lane_of == 1, middle, jnp.where(lane_of == 2, small, zero))
            )
            do_t[:, rows] = dot(eye, grad_out, ((1,), (1,))).astype(jnp.bfloat16)
            q_t[:, rows] = dot(eye, wide[rows, Q0:K0], ((1,), (1,))).astype(jnp.bfloat16)
            parts = jnp.concatenate(split(og[rows, :].astype(jnp.float32) * attention), axis=1)
            sums = dot(step_hot[:, rows], parts, ((1,), (0,)))
            return step_total + ((sums[:, 2 * HEAD :] + sums[:, HEAD : 2 * HEAD]) + sums[:, :HEAD])

        before = None
        for n in range(N_Z):
            rows = zs_rows(n)
            row_top = jnp.max(top, axis=1, keepdims=True)
            top = None
            if n + 1 < N_Z:
                queries = query_rows(n + 1)
            summed = None
            for t in range(SEQ // TILE):
                columns = slice(t * TILE, (t + 1) * TILE)
                if n + 1 < N_Z:
                    top = score_tile(n + 1, t, queries, top)
                parts = jnp.exp2((scores[n % 2][:, columns] - row_top) * SCALE2).astype(jnp.bfloat16)
                weights[rows, columns] = parts
                term = dot(parts, wide[columns, V0 : V0 + 2 * HEAD], ((1,), (0,)))
                summed = term if summed is None else summed + term
                if t == 0 and before is not None:
                    step_total = finish_rows(n - 1, before, step_total)
            before = summed
        step_total = finish_rows(N_Z - 1, before, step_total)

        for p in range(8):
            gpart[p] = step_total[8 * p : 8 * p + 8, :]
        owner_blk = jnp.where(core == 1, blk, other_blk)
        for n in range(8):
            copy = remote(
                gpart.at[halves[n]], g1.at[dp], g1s, g1r, halves[n] * 2 + 1, owner_blk
            )
            if n:
                copy.start()
            else:
                pl.when(core == 0)(copy.start)

        @pl.when(core == 1)
        def _():
            g1[pl.ds(dp, 1)] = gpart[pl.ds(halves[0], 1)]

        for n in range(N_Z):
            rows = zs_rows(n)
            up = grads_up[rows, :]
            for t in range(SEQ // TILE):
                columns = slice(t * TILE, (t + 1) * TILE)
                prob_grad = dot(up, wide[columns, V0 : V0 + 2 * HEAD], ((1,), (1,)))
                dscore[rows, columns] = (weights[rows, columns].astype(jnp.float32) * prob_grad).astype(jnp.bfloat16)
            query_grad = dot(dscore[rows, :], wide[:, K0:U0], ((1,), (0,))) * SCALE
            cbuf[zs_rows(n, 1), :] = query_grad.astype(jnp.bfloat16)
            pl.when(core == 1)(lambda: send_back(1, n))

        def finish_steps():
            wait_for(g1.at[pl.ds(0, 15)], g1r)
            g2[halves[0], head] = jnp.sum(g1[...], axis=0)
            mine = g2.at[halves[0], head]
            for n in range(1, N_BLK):
                remote(mine, mine, g2s, g2r, dp, lax.rem(blk + n, N_BLK)).start()

        @pl.when(core == 1)
        def _():
            finish_steps()

        for n in range(N_Z):
            columns = zs_rows(n)
            key_grad = dot(q_t[...], dscore[:, columns], ((1,), (0,))) * SCALE
            cbuf[zs_rows(n, 2), :] = key_grad.T.astype(jnp.bfloat16)
            value_grad = dot(do_t[...], weights[:, columns], ((1,), (0,)))
            cbuf[zs_rows(n, 3), :] = value_grad.T.astype(jnp.bfloat16)

            @pl.when(core == 1)
            def _():
                send_back(2, n)
                send_back(3, n)

    @pl.when(core == 0)
    def _():
        pl.semaphore_wait(go, 1)

        @pl.when(is_host)
        def _():
            for n in range(N_Z):
                for which in range(4):
                    send_back(which, n)

    @pl.when(core == 1)
    def _():
        @pl.when(is_host)
        def _():
            wait_for(g2.at[halves[0], pl.ds(0, 11)], g2r)

        @pl.when(jnp.logical_not(is_host))
        def _():
            wait_for(g2.at[halves[0]], g2r)

        mine = g2.at[halves[0]]
        for n in range(16):
            dp_to = halves[n // 2] * 2 + cores[n % 2]
            if n:
                remote(mine, mine, g3s, g3r, dp_to, blk).start()

    wait_for(slot_dst.at[pl.ds(0, 31)], sl_send)
    wait_for(stage.at[pl.ds(0, 186 * CAP), :], a_send)
    @pl.when(core == 0)
    def _():
        wait_for(g2.at[pl.ds(0, 8)], g3r)

    @pl.when(core == 1)
    def _():
        wait_for(g2.at[pl.ds(0, 7)], g3r)

    for p in range(8):
        for h in range(HEADS):
            gg_ref[8 * p : 8 * p + 8, h * HEAD : (h + 1) * HEAD] = g2[p, h]

    @pl.when(is_host)
    def _():
        wait_for(grad_ref.at[:, pl.ds(0, 11 * HEAD)], do_send)

        @pl.when(core == 0)
        def _():
            wait_for(bsend.at[pl.ds(0, 5 * ROWS), :], b_send)


        @pl.when(core == 0)
        def _():
            wait_for(gpart.at[pl.ds(0, 8)], g1s)

        @pl.when(core == 1)
        def _():
            wait_for(gpart.at[pl.ds(0, 7)], g1s)
            wait_for(g1.at[pl.ds(0, 15)], g2s)

        wait_for(att_ref.at[:, pl.ds(0, 11 * HEAD)], ca_recv)
        wait_for(qkvg_ref.at[:, pl.ds(0, 33 * HEAD)], cq_recv)
        wait_for(cbuf.at[pl.ds(0, 60 * TOK), :], c_send)

    @pl.when(jnp.logical_not(is_host))
    def _():
        wait_for(grad_ref, do_send)

        @pl.when(core == 0)
        def _():
            wait_for(bsend, b_send)

        wait_for(att_ref, ca_recv)
        wait_for(qkvg_ref, cq_recv)

    @pl.when(core == 1)
    def _():
        wait_for(stage.at[pl.ds(0, 960), :], g3s)


def local(rows_in, slot_rows, clip_ids, clip_reach, clip_step, gate_table, out_grad):
    vmem = pl.BlockSpec(memory_space=pltpu.VMEM)
    smem = pl.BlockSpec(memory_space=pltpu.SMEM)
    bf16, f32 = jnp.bfloat16, jnp.float32
    sem = pltpu.SemaphoreType.DMA
    attended, qkv_grad, gate_grad = pl.pallas_call(
        kernel,
        out_shape=(
            jax.ShapeDtypeStruct((TOK, WIDTH), bf16),
            jax.ShapeDtypeStruct((TOK, 3 * WIDTH), bf16),
            jax.ShapeDtypeStruct((STEPS, WIDTH), f32),
        ),
        in_specs=[vmem, vmem, vmem, smem, smem, vmem, vmem],
        out_specs=(vmem, vmem, vmem),
        scratch_shapes=[
            pltpu.VMEM((CHUNKS * 2 * N_DP * CAP, SPAN), bf16),
            pltpu.VMEM((CHUNKS * 2 * SLOTS, SPAN), bf16),
            pltpu.VMEM((N_DP, 1, SLOTS), f32),
            pltpu.VMEM((2 * N_DP, 1, SLOTS), f32),
            pltpu.VMEM((CHUNKS * ROWS, SPAN), bf16),
            pltpu.VMEM((SEQ, 5 * HEAD), bf16),
            pltpu.VMEM((SEQ, HEAD), bf16),
            pltpu.VMEM((SEQ, HEAD), bf16),
            pltpu.VMEM((SEQ, HEAD), bf16),
            pltpu.VMEM((SEQ, HEAD), bf16),
            pltpu.VMEM((SEQ, 2 * HEAD), bf16),
            pltpu.VMEM((STEPS, SEQ), bf16),
            pltpu.VMEM((SEQ, SEQ), bf16),
            pltpu.VMEM((SEQ, SEQ), bf16),
            pltpu.VMEM((ROWS, SEQ), f32),
            pltpu.VMEM((ROWS, SEQ), f32),
            pltpu.VMEM((HEAD, SEQ), bf16),
            pltpu.VMEM((HEAD, SEQ), bf16),
            pltpu.VMEM((4 * SEQ, HEAD), bf16),
            pltpu.VMEM((8, 8, HEAD), f32),
            pltpu.VMEM((N_DP, 8, HEAD), f32),
            pltpu.VMEM((8, HEADS, 8, HEAD), f32),
            sem, sem((CHUNKS,)), sem, sem, sem, sem, sem, sem, sem, sem, sem,
            sem, sem, sem, sem, sem, sem, pltpu.SemaphoreType.REGULAR,
        ],
        compiler_params=pltpu.CompilerParams(
            collective_id=0, has_side_effects=True, vmem_limit_bytes=56 * 2**20
        ),
        name="attention",
    )(
        rows_in.reshape(8, 2, CAP, 3 * WIDTH),
        slot_rows.reshape(N_DP, CAP),
        clip_ids,
        clip_reach,
        clip_step,
        gate_table,
        out_grad[0],
    )
    return attended[None], qkv_grad[None], gate_grad


def solution(mesh):
    return jax.shard_map(
        local,
        mesh=mesh,
        in_specs=(
            P("dp", "blk", None, None, None),
            P("dp", "blk", None, None),
            P("dp", None),
            P("dp", None),
            P("dp", None),
            P(),
            P("dp", "blk", None),
        ),
        out_specs=(P("dp", "blk", None), P("dp", "blk", None), P()),
        check_vma=False,
    )
```

time: 123 us -> 107 us (0.87)
  the two profiles are of different devices: /device:TPU:1 before, /device:TPU:4 now
where the time goes in v2:
time: 107 us
  Pallas kernels  101 us (94%)
  local copies, waits for them, and re-layouts  4.93 us (5%)
    pallas_call x1, Pallas kernels, local(): pl.pallas_call(kernel, out_shape=(jax.ShapeDtypeStruct((TOK, WIDTH), bf16...  101 us
    unnamed x5, local copies, waits for them, and re-layouts  4.93 us

profile of v2, /device:TPU:4, one launch (start us, length us, event | category | flops | bytes accessed | tf_op | source)
XLA Modules:
  0.0 106.9 jit_solution(10987780319098618422)
XLA Ops:
  0.6 101.3 %attention.1 = (bf16[128,1536]{1,0:T(8,128)(2,1)}, bf16[128,4608]{1,0:T(8,128)(2,1)}, f32[64,1536]{1,0:T(8,128)}) custom-call(bf16[8,2,16,4608]{3,2,1,0:T(8,128)(2,1)} %bitcast.5, s32[16,16]{1,0:T(8,128)} %bitcast.9, s32[1,2048]{1,0:T(1,128)} %clip_ref.1, s32[1,4]{1,0:T(1,128)} %reach_ref.1, s32[1,4]{1,0:T(1,128)} %step_ref.1, bf16[64,1536]{1,0:T(8,128)(2,1)} %gate_ref.1, ...), custom_call_target="tpu_custom_call" | custom-call | tf_op jit(solution)/shard_map/attention/pallas_call | solution.py:525
  102.0 1.8 %copy.13 = bf16[1,128,1536]{2,1,0:T(8,128)(2,1)} copy(bf16[1,128,1536]{2,1,0:T(8,128)(2,1)} %bitcast.7) | data formatting | bytes 786432
  103.7 0.0 copy-start
  103.7 2.4 %copy.14 = bf16[1,128,4608]{2,1,0:T(8,128)(2,1)} copy(bf16[1,128,4608]{2,1,0:T(8,128)(2,1)} %bitcast.6) | data formatting | bytes 2359296
  106.1 0.0 copy-done
  106.1 0.7 copy.15
Async XLA Ops:
  103.7 2.4 %copy-start = (f32[64,1536]{1,0:T(8,128)S(1)}, f32[64,1536]{1,0:T(8,128)}, u32[]{:S(2)}) copy-start(f32[64,1536]{1,0:T(8,128)} %get-tuple-element.14) | copy-start | bytes 1179652

commit v3 on v2

--- a/solution.py
+++ b/solution.py
@@ -67,7 +67,7 @@
     stage, recv, slot_src, slot_dst, bsend, wide, og, units, gates, grads, grads_up, step_hot,
     weights, dscore, scores_a, scores_b, q_t, do_t, cbuf, gpart, g1, g2,
     a_send, a_recv, sl_send, sl_recv, do_send, do_recv, b_send, b_recv, c_send, ca_recv, cq_recv,
-    g1s, g1r, g2s, g2r, g3s, g3r, go,
+    g1s, g1r, g2s, g2r, g3s, g3r,
 ):
     dp = lax.axis_index("dp")
     blk = lax.axis_index("blk")
@@ -159,8 +159,8 @@
     source_row = source * CAP
     targets = [x_tos[n % 2] * 256 + halves[n // 2] * CAP for n in range(16)]
 
-    for core_to in (0, 1):
-        for k in range(CHUNKS):
+    for k in range(CHUNKS):
+        for core_to in (0, 1):
             for n in range(16):
                 copy = remote(
                     stage.at[pl.ds(pl.multiple_of(targets[n] + (k * 512 + core_to * 128), CAP), CAP), :],
@@ -299,18 +299,6 @@
                 def _():
                     place[...] = block[...]
 
-    @pl.when(core == 1)
-    def _():
-        @pl.when(is_host)
-        def _():
-            wait_for(bsend.at[pl.ds(0, 5 * ROWS), :], b_send)
-
-        @pl.when(jnp.logical_not(is_host))
-        def _():
-            wait_for(bsend, b_send)
-
-        pl.semaphore_signal(go, inc=1, device_id=(halves[0] * 2, blk), device_id_type=MESH)
-
     @pl.when(is_host)
     def _():
         wait_for(og.at[pl.ds(0, 15 * TOK), :], do_recv)
@@ -352,7 +340,7 @@
             inverse = 1.0 / summed[:, HEAD:]
             attention = summed[:, :HEAD] * inverse
             cbuf[zs_rows(n), :] = (gates[rows, :].astype(jnp.float32) * attention).astype(jnp.bfloat16)
-            pl.when(core == 1)(lambda: send_back(0, n))
+            send_back(0, n)
             grad_out = grads[rows, :].astype(jnp.float32)
             row_delta = jnp.sum(grad_out * attention, axis=1, keepdims=True) * inverse
             grad_out = (grad_out * inverse).astype(jnp.bfloat16)
@@ -414,7 +402,7 @@
                 dscore[rows, columns] = (weights[rows, columns].astype(jnp.float32) * prob_grad).astype(jnp.bfloat16)
             query_grad = dot(dscore[rows, :], wide[:, K0:U0], ((1,), (0,))) * SCALE
             cbuf[zs_rows(n, 1), :] = query_grad.astype(jnp.bfloat16)
-            pl.when(core == 1)(lambda: send_back(1, n))
+            send_back(1, n)
 
         def finish_steps():
             wait_for(g1.at[pl.ds(0, 15)], g1r)
@@ -434,20 +422,8 @@
             value_grad = dot(do_t[...], weights[:, columns], ((1,), (0,)))
             cbuf[zs_rows(n, 3), :] = value_grad.T.astype(jnp.bfloat16)
 
-            @pl.when(core == 1)
-            def _():
-                send_back(2, n)
-                send_back(3, n)
-
-    @pl.when(core == 0)
-    def _():
-        pl.semaphore_wait(go, 1)
-
-        @pl.when(is_host)
-        def _():
-            for n in range(N_Z):
-                for which in range(4):
-                    send_back(which, n)
+            send_back(2, n)
+            send_back(3, n)
 
     @pl.when(core == 1)
     def _():
@@ -482,11 +458,7 @@
     @pl.when(is_host)
     def _():
         wait_for(grad_ref.at[:, pl.ds(0, 11 * HEAD)], do_send)
-
-        @pl.when(core == 0)
-        def _():
-            wait_for(bsend.at[pl.ds(0, 5 * ROWS), :], b_send)
-
+        wait_for(bsend.at[pl.ds(0, 5 * ROWS), :], b_send)
 
         @pl.when(core == 0)
         def _():
@@ -504,17 +476,19 @@
     @pl.when(jnp.logical_not(is_host))
     def _():
         wait_for(grad_ref, do_send)
-
-        @pl.when(core == 0)
-        def _():
-            wait_for(bsend, b_send)
-
+        wait_for(bsend, b_send)
         wait_for(att_ref, ca_recv)
         wait_for(qkvg_ref, cq_recv)
 
     @pl.when(core == 1)
     def _():
         wait_for(stage.at[pl.ds(0, 960), :], g3s)
+
+
+def settle(a, b, c, a_out, b_out, c_out):
+    a_out[...] = a[...]
+    b_out[...] = b[...]
+    c_out[...] = c[...]
 
 
 def local(rows_in, slot_rows, clip_ids, clip_reach, clip_step, gate_table, out_grad):
@@ -555,7 +529,7 @@
             pltpu.VMEM((N_DP, 8, HEAD), f32),
             pltpu.VMEM((8, HEADS, 8, HEAD), f32),
             sem, sem((CHUNKS,)), sem, sem, sem, sem, sem, sem, sem, sem, sem,
-            sem, sem, sem, sem, sem, sem, pltpu.SemaphoreType.REGULAR,
+            sem, sem, sem, sem, sem, sem,
         ],
         compiler_params=pltpu.CompilerParams(
             collective_id=0, has_side_effects=True, vmem_limit_bytes=56 * 2**20
@@ -570,6 +544,16 @@
         gate_table,
         out_grad[0],
     )
+    shapes = [x.shape for x in (attended, qkv_grad, gate_grad)]
+    blocks = [pl.BlockSpec((rows // 4, columns), lambda i: (i, 0)) for rows, columns in shapes]
+    attended, qkv_grad, gate_grad = pl.pallas_call(
+        settle,
+        grid=(4,),
+        out_shape=tuple(jax.ShapeDtypeStruct(x.shape, x.dtype) for x in (attended, qkv_grad, gate_grad)),
+        in_specs=blocks,
+        out_specs=tuple(blocks),
+        name="settle",
+    )(attended, qkv_grad, gate_grad)
     return attended[None], qkv_grad[None], gate_grad
 
 

time: 107 us -> 102 us (0.953)
  the two profiles are of different devices: /device:TPU:4 before, /device:TPU:1 now
where the time goes in v3:
time: 102 us
  Pallas kernels  101 us (99%)
    pallas_call x1, Pallas kernels, local(): pl.pallas_call(kernel, out_shape=(jax.ShapeDtypeStruct((TOK, WIDTH), bf16...  97.8 us
    pallas_call x1, Pallas kernels, local(): pl.pallas_call(settle, grid=(4,), out_shape=tuple((jax.ShapeDtypeStruct(x...  3.69 us

profile of v3, /device:TPU:1, one launch (start us, length us, event | category | flops | bytes accessed | tf_op | source)
XLA Modules:
  0.0 102.1 jit_solution(17601070367085312434)
XLA Ops:
  0.6 97.8 %attention.1 = (bf16[128,1536]{1,0:T(8,128)(2,1)}, bf16[128,4608]{1,0:T(8,128)(2,1)}, f32[64,1536]{1,0:T(8,128)}) custom-call(bf16[8,2,16,4608]{3,2,1,0:T(8,128)(2,1)} %bitcast.5, s32[16,16]{1,0:T(8,128)} %bitcast.7, s32[1,2048]{1,0:T(1,128)} %clip_ref.1, s32[1,4]{1,0:T(1,128)} %reach_ref.1, s32[1,4]{1,0:T(1,128)} %step_ref.1, bf16[64,1536]{1,0:T(8,128)(2,1)} %gate_ref.1, ...), custom_call_target="tpu_custom_call" | custom-call | tf_op jit(solution)/shard_map/attention/pallas_call | solution.py:499
  98.4 3.7 %settle.1 = (bf16[128,1536]{1,0:T(8,128)(2,1)}, bf16[128,4608]{1,0:T(8,128)(2,1)}, f32[64,1536]{1,0:T(8,128)}) custom-call(bf16[128,1536]{1,0:T(8,128)(2,1)} %get-tuple-element.9.a, bf16[128,4608]{1,0:T(8,128)(2,1)} %get-tuple-element.10.b, f32[64,1536]{1,0:T(8,128)} %get-tuple-element.11.c), custom_call_target="tpu_custom_call" | custom-call | tf_op jit(solution)/shard_map/settle/pallas_call | solution.py:549

commit v4 on v3

--- a/solution.py
+++ b/solution.py
@@ -29,6 +29,7 @@
 SCALE2 = SCALE * math.log2(math.e)
 NEGATIVE = -1e30
 Q0, K0, U0, V0, ONE0 = 0, 128, 256, 384, 512
+GATE_AT = 4
 RETURNS = (4, 3, 5, 2, 6, 1, 7, 0)
 ORDER = ((3, 5, 2, 6, 1, 7), (4, 3, 2, 6, 7, 0), (4, 3, 5, 1, 7, 0), (4, 5, 2, 6, 1, 0))
 
@@ -64,11 +65,13 @@
 def kernel(
     rows_ref, slot_ref, clip_ref, reach_ref, step_ref, gate_ref, grad_ref,
     att_ref, qkvg_ref, gg_ref,
-    stage, recv, slot_src, slot_dst, bsend, wide, og, units, gates, grads, grads_up, step_hot,
+    rows_here, in_sem, stage, recv, slot_src, slot_dst, bsend, wide, og, units, gates, grads, grads_up, step_hot,
     weights, dscore, scores_a, scores_b, q_t, do_t, cbuf, gpart, g1, g2,
     a_send, a_recv, sl_send, sl_recv, do_send, do_recv, b_send, b_recv, c_send, ca_recv, cq_recv,
-    g1s, g1r, g2s, g2r, g3s, g3r,
+    g1s, g1r, g2s, g2r, g3s, g3r, hop,
 ):
+    for n in range(8):
+        pltpu.make_async_copy(rows_ref.at[n], rows_here.at[n], in_sem).start()
     dp = lax.axis_index("dp")
     blk = lax.axis_index("blk")
     far_x = dp // 8
@@ -117,6 +120,7 @@
     def stage_base(k, x_to, core_to):
         return ((k * 2 + x_to) * 2 + core_to) * 128
 
+    wait_for(rows_here, in_sem)
     for core_to in (0, 1):
         for k in range(CHUNKS):
             for x_to in (0, 1):
@@ -125,7 +129,7 @@
                 column = pl.multiple_of((x_to * CHUNKS + rank_of(z_to, far)) * HEAD, HEAD)
                 base = stage_base(k, x_to, core_to)
                 for part in range(3):
-                    stage[base : base + 128, part * HEAD : (part + 1) * HEAD] = rows_ref[
+                    stage[base : base + 128, part * HEAD : (part + 1) * HEAD] = rows_here[
                         :, core_to, :, pl.ds(part * WIDTH + column, HEAD)
                     ].reshape(128, HEAD)
 
@@ -279,25 +283,59 @@
         base = lax.rem(z + RETURNS[n], N_Z) * ROWS
         return pl.ds(pl.multiple_of(which * SEQ + base, ROWS), ROWS)
 
+    relayed = lax.rem(z, 4) == skip_of(core, 1 - x_lo)
+    relayed_head = (1 - x_lo) * CHUNKS + rank_of(z, skip_of(core, 1 - x_lo))
+
+    def back_place(which, of_head):
+        target, column = ((att_ref, 0), (qkvg_ref, 0), (qkvg_ref, 1), (qkvg_ref, 2))[which]
+        return target.at[:, pl.ds(pl.multiple_of(column * WIDTH + of_head * HEAD, HEAD), HEAD)]
+
+    def back_block(which, z_to, half):
+        return cbuf.at[pl.ds(pl.multiple_of(which * SEQ + z_to * ROWS + half * TOK, TOK), TOK), :]
+
     def send_back(which, n):
-        target, column, arrive = (
-            (att_ref, 0, ca_recv), (qkvg_ref, 0, cq_recv), (qkvg_ref, 1, cq_recv), (qkvg_ref, 2, cq_recv)
-        )[which]
+        arrive = cq_recv if which else ca_recv
         z_to = lax.rem(z + RETURNS[n], N_Z)
-        place = target.at[:, pl.ds(pl.multiple_of(column * WIDTH + head * HEAD, HEAD), HEAD)]
-        for half in range(2):
-            block = cbuf.at[
-                pl.ds(pl.multiple_of(which * SEQ + z_to * ROWS + half * TOK, TOK), TOK), :
-            ]
-            copy = remote(block, place, c_send, arrive, dp, z_to * 2 + half)
-            if RETURNS[n]:
-                copy.start()
-            else:
-                pl.when(half != x_lo)(copy.start)
-
-                @pl.when(half == x_lo)
+        place = back_place(which, head)
+        near = back_block(which, z_to, x_lo)
+        far = back_block(which, z_to, 1 - x_lo)
+        straight = remote(far, place, c_send, arrive, dp, z_to * 2 + 1 - x_lo)
+        if RETURNS[n]:
+            remote(near, place, c_send, arrive, dp, z_to * 2 + x_lo).start()
+            by_relay = remote(far, far, c_send, hop.at[which * 8 + n], dp, blk_tos[1])
+            pl.when(relayed)(by_relay.start)
+            pl.when(jnp.logical_not(relayed))(straight.start)
+        else:
+            place[...] = near[...]
+            straight.start()
+
+    def pass_steps():
+        mine = g2.at[halves[0]]
+        for n in range(1, 16):
+            remote(mine, mine, g3s, g3r, halves[n // 2] * 2 + cores[n % 2], blk).start()
+
+    def pass_on(which, n):
+        z_to = lax.rem(z + RETURNS[n], N_Z)
+        block = back_block(which, z_to, x_lo)
+        wait_for(block, hop.at[which * 8 + n])
+        arrive = cq_recv if which else ca_recv
+        remote(block, back_place(which, relayed_head), c_send, arrive, dp, z_to * 2 + x_lo).start()
+
+    @pl.when(jnp.logical_not(is_host))
+    def _():
+        for which in range(2):
+            for n in range(N_Z - 1):
+                pass_on(which, n)
+        for n in range(N_Z - 1):
+            if n == GATE_AT:
+
+                @pl.when(core == 1)
                 def _():
-                    place[...] = block[...]
+                    wait_for(g2.at[halves[0]], g2r)
+                    pass_steps()
+
+            pass_on(2, n)
+            pass_on(3, n)
 
     @pl.when(is_host)
     def _():
@@ -425,21 +463,10 @@
             send_back(2, n)
             send_back(3, n)
 
-    @pl.when(core == 1)
-    def _():
-        @pl.when(is_host)
-        def _():
-            wait_for(g2.at[halves[0], pl.ds(0, 11)], g2r)
-
-        @pl.when(jnp.logical_not(is_host))
-        def _():
-            wait_for(g2.at[halves[0]], g2r)
-
-        mine = g2.at[halves[0]]
-        for n in range(16):
-            dp_to = halves[n // 2] * 2 + cores[n % 2]
-            if n:
-                remote(mine, mine, g3s, g3r, dp_to, blk).start()
+    @pl.when((core == 1) & is_host)
+    def _():
+        wait_for(g2.at[halves[0], pl.ds(0, 11)], g2r)
+        pass_steps()
 
     wait_for(slot_dst.at[pl.ds(0, 31)], sl_send)
     wait_for(stage.at[pl.ds(0, 186 * CAP), :], a_send)
@@ -477,6 +504,7 @@
     def _():
         wait_for(grad_ref, do_send)
         wait_for(bsend, b_send)
+        wait_for(cbuf.at[pl.ds(0, 28 * TOK), :], c_send)
         wait_for(att_ref, ca_recv)
         wait_for(qkvg_ref, cq_recv)
 
@@ -503,9 +531,11 @@
             jax.ShapeDtypeStruct((TOK, 3 * WIDTH), bf16),
             jax.ShapeDtypeStruct((STEPS, WIDTH), f32),
         ),
-        in_specs=[vmem, vmem, vmem, smem, smem, vmem, vmem],
+        in_specs=[pl.BlockSpec(memory_space=pl.ANY), vmem, vmem, smem, smem, vmem, vmem],
         out_specs=(vmem, vmem, vmem),
         scratch_shapes=[
+            pltpu.VMEM((8, 2, CAP, 3 * WIDTH), bf16),
+            sem,
             pltpu.VMEM((CHUNKS * 2 * N_DP * CAP, SPAN), bf16),
             pltpu.VMEM((CHUNKS * 2 * SLOTS, SPAN), bf16),
             pltpu.VMEM((N_DP, 1, SLOTS), f32),
@@ -529,7 +559,7 @@
             pltpu.VMEM((N_DP, 8, HEAD), f32),
             pltpu.VMEM((8, HEADS, 8, HEAD), f32),
             sem, sem((CHUNKS,)), sem, sem, sem, sem, sem, sem, sem, sem, sem,
-            sem, sem, sem, sem, sem, sem,
+            sem, sem, sem, sem, sem, sem, sem((32,)),
         ],
         compiler_params=pltpu.CompilerParams(
             collective_id=0, has_side_effects=True, vmem_limit_bytes=56 * 2**20
@@ -545,10 +575,10 @@
         out_grad[0],
     )
     shapes = [x.shape for x in (attended, qkv_grad, gate_grad)]
-    blocks = [pl.BlockSpec((rows // 4, columns), lambda i: (i, 0)) for rows, columns in shapes]
+    blocks = [pl.BlockSpec((rows // 2, columns), lambda i: (i, 0)) for rows, columns in shapes]
     attended, qkv_grad, gate_grad = pl.pallas_call(
         settle,
-        grid=(4,),
+        grid=(2,),
         out_shape=tuple(jax.ShapeDtypeStruct(x.shape, x.dtype) for x in (attended, qkv_grad, gate_grad)),
         in_specs=blocks,
         out_specs=tuple(blocks),

time: 102 us -> 96.2 us (0.943)
  Pallas kernels: 101 us -> 95.2 us
    pallas_call x1, Pallas kernels: 97.8 us -> 92.7 us  [local(): pl.pallas_call(kernel, out_shape=(jax.ShapeDtypeStruct((TOK, WIDTH), bf16...]
    pallas_call x1, Pallas kernels: 3.69 us -> 2.5 us  [local(): pl.pallas_call(settle, grid=(2,), out_shape=tuple((jax.ShapeDtypeStruct(x...]
where the time goes in v4:
time: 96.2 us; the launch traced here: 95.8 us
  Pallas kernels  95.2 us (99%)
    pallas_call x1, Pallas kernels, local(): pl.pallas_call(kernel, out_shape=(jax.ShapeDtypeStruct((TOK, WIDTH), bf16...  92.7 us
    pallas_call x1, Pallas kernels, local(): pl.pallas_call(settle, grid=(2,), out_shape=tuple((jax.ShapeDtypeStruct(x...  2.5 us

profile of v4, /device:TPU:1, one launch (start us, length us, event | category | flops | bytes accessed | tf_op | source)
XLA Modules:
  0.0 95.8 jit_solution(4207185743512656187)
XLA Ops:
  0.6 92.7 %attention.1 = (bf16[128,1536]{1,0:T(8,128)(2,1)}, bf16[128,4608]{1,0:T(8,128)(2,1)}, f32[64,1536]{1,0:T(8,128)}) custom-call(bf16[8,2,16,4608]{3,2,1,0:T(8,128)(2,1)} %bitcast.5, s32[16,16]{1,0:T(8,128)} %bitcast.7, s32[1,2048]{1,0:T(1,128)} %clip_ref.1, s32[1,4]{1,0:T(1,128)} %reach_ref.1, s32[1,4]{1,0:T(1,128)} %step_ref.1, bf16[64,1536]{1,0:T(8,128)(2,1)} %gate_ref.1, ...), custom_call_target="tpu_custom_call" | custom-call | tf_op jit(solution)/shard_map/attention/pallas_call | solution.py:527
  93.3 2.5 %settle.1 = (bf16[128,1536]{1,0:T(8,128)(2,1)}, bf16[128,4608]{1,0:T(8,128)(2,1)}, f32[64,1536]{1,0:T(8,128)}) custom-call(bf16[128,1536]{1,0:T(8,128)(2,1)} %get-tuple-element.9.a, bf16[128,4608]{1,0:T(8,128)(2,1)} %get-tuple-element.10.b, f32[64,1536]{1,0:T(8,128)} %get-tuple-element.11.c), custom_call_target="tpu_custom_call" | custom-call | tf_op jit(solution)/shard_map/settle/pallas_call | solution.py:579

commit v5 on v4

--- a/solution.py
+++ b/solution.py
@@ -30,7 +30,7 @@
 NEGATIVE = -1e30
 Q0, K0, U0, V0, ONE0 = 0, 128, 256, 384, 512
 GATE_AT = 4
-RETURNS = (4, 3, 5, 2, 6, 1, 7, 0)
+RETURNS = (1, 7, 2, 6, 3, 5, 4, 0)
 ORDER = ((3, 5, 2, 6, 1, 7), (4, 3, 2, 6, 7, 0), (4, 3, 5, 1, 7, 0), (4, 5, 2, 6, 1, 0))
 
 

time: 96.2 us -> 97.4 us (1.012)
  Pallas kernels: 95.2 us -> 96.6 us
    pallas_call x1, Pallas kernels: 92.7 us -> 94.1 us  [local(): pl.pallas_call(kernel, out_shape=(jax.ShapeDtypeStruct((TOK, WIDTH), bf16...]
where the time goes in v5:
time: 97.4 us; the launch traced here: 97.2 us
  Pallas kernels  96.6 us (99%)
    pallas_call x1, Pallas kernels, local(): pl.pallas_call(kernel, out_shape=(jax.ShapeDtypeStruct((TOK, WIDTH), bf16...  94.1 us
    pallas_call x1, Pallas kernels, local(): pl.pallas_call(settle, grid=(2,), out_shape=tuple((jax.ShapeDtypeStruct(x...  2.5 us

profile of v5, /device:TPU:1, one launch (start us, length us, event | category | flops | bytes accessed | tf_op | source)
XLA Modules:
  0.0 97.2 jit_solution(10257959177113363074)
XLA Ops:
  0.6 94.1 %attention.1 = (bf16[128,1536]{1,0:T(8,128)(2,1)}, bf16[128,4608]{1,0:T(8,128)(2,1)}, f32[64,1536]{1,0:T(8,128)}) custom-call(bf16[8,2,16,4608]{3,2,1,0:T(8,128)(2,1)} %bitcast.5, s32[16,16]{1,0:T(8,128)} %bitcast.7, s32[1,2048]{1,0:T(1,128)} %clip_ref.1, s32[1,4]{1,0:T(1,128)} %reach_ref.1, s32[1,4]{1,0:T(1,128)} %step_ref.1, bf16[64,1536]{1,0:T(8,128)(2,1)} %gate_ref.1, ...), custom_call_target="tpu_custom_call" | custom-call | tf_op jit(solution)/shard_map/attention/pallas_call | solution.py:527
  94.7 2.5 %settle.1 = (bf16[128,1536]{1,0:T(8,128)(2,1)}, bf16[128,4608]{1,0:T(8,128)(2,1)}, f32[64,1536]{1,0:T(8,128)}) custom-call(bf16[128,1536]{1,0:T(8,128)(2,1)} %get-tuple-element.9.a, bf16[128,4608]{1,0:T(8,128)(2,1)} %get-tuple-element.10.b, f32[64,1536]{1,0:T(8,128)} %get-tuple-element.11.c), custom_call_target="tpu_custom_call" | custom-call | tf_op jit(solution)/shard_map/settle/pallas_call | solution.py:579
